TPU v7x, 32 devices: a whole 2x2x4 slice. The times are simulated.
32 devices in a mesh: slab: 8 (over z, x), mode: 4 (over y, core).
Axes of the slice: x: 2, y: 2, z: 4, core: 2. Of those that a mesh axis runs over, the one named last changes fastest.
Arguments:
- design: float32 [16, 128, 128], P('slab', 'mode'), may hold values from 0.03 to 1
- mode_shapes: float32 [4, 3, 16, 128, 128], P('mode', None, 'slab'), may hold values from -2.4 to 2.4
- eigenvalues: float32 [4], P('mode'), may hold values from 0.5 to 2
Outputs:
- sensitivity: float32 [16, 128, 128], P('slab', 'mode')
- new_design: float32 [16, 128, 128], P('slab', 'mode')
All inputs are finite; a program needn't handle non-finite values.
Results may differ from a plain program's by a relative error of at most 0.0003.
Values sent between devices are 32-bit elements; how exact they have to be, the bound alone decides.
A program may use at most 64 MiB of HBM per device.

v0:
```python
import jax
import jax.numpy as jnp
import numpy as np
from jax import lax
from jax.sharding import PartitionSpec as P

FR = 3
BISECT = 12


KS_SHARP = 2.0
PENALTY = 3.0
FLOOR_MODULUS = 0.001
MOVE_LIMIT = 0.2
POISSON = 0.3
LEVEL_LOW = -14.0
LEVEL_HIGH = 14.0


def padded_2(value, sides, width):
    for axis, dim in sides:
        count, length = (lax.axis_size(axis), value.shape[dim])
        up = [(i, (i + 1) % count) for i in range(count - 1)]
        down = [(j, i) for i, j in up]
        last = lax.slice_in_dim(value, length - width, length, axis=dim)
        leading = lax.slice_in_dim(value, 0, width, axis=dim)
        before = lax.ppermute(last, axis, up)
        after = lax.ppermute(leading, axis, down)
        value = jnp.concatenate([before, value, after], axis=dim)
    return value


def shifted_2(value, axis, by):
    count = lax.axis_size(axis)
    pairs = [(i, i + by) for i in range(count) if 0 <= i + by < count]
    return lax.ppermute(value, axis, pairs)


def element_tables():
    lame_first = POISSON / ((1.0 + POISSON) * (1.0 - 2.0 * POISSON))
    shear_modulus = 0.5 / (1.0 + POISSON)
    elastic = np.zeros((6, 6))
    elastic[:3, :3] = lame_first
    for i in range(3):
        elastic[i, i] += 2.0 * shear_modulus
        elastic[i + 3, i + 3] = shear_modulus
    corner_signs = np.array([[a, b, c] for a in (0, 1) for b in (0, 1) for c in (0, 1)]) * 2.0 - 1.0
    gauss_points = [-1.0 / np.sqrt(3.0), 1.0 / np.sqrt(3.0)]
    stiffness = np.zeros((24, 24))
    mass_matrix = np.zeros((24, 24))
    for first in gauss_points:
        for second in gauss_points:
            for third in gauss_points:
                sample = np.array([first, second, third])
                factors = 1.0 + corner_signs * sample
                shape_values = np.prod(factors, axis=1) / 8.0
                gradients = np.zeros((8, 3))
                for d in range(3):
                    others = [e for e in range(3) if e != d]
                    gradients[:, d] = (
                        corner_signs[:, d] * factors[:, others[0]] * factors[:, others[1]] / 4.0
                    )
                strain = np.zeros((6, 24))
                shape_rows = np.zeros((3, 24))
                for n in range(8):
                    strain[0, 3 * n] = gradients[n, 0]
                    strain[1, 3 * n + 1] = gradients[n, 1]
                    strain[2, 3 * n + 2] = gradients[n, 2]
                    strain[3, 3 * n] = gradients[n, 1]
                    strain[3, 3 * n + 1] = gradients[n, 0]
                    strain[4, 3 * n + 1] = gradients[n, 2]
                    strain[4, 3 * n + 2] = gradients[n, 1]
                    strain[5, 3 * n] = gradients[n, 2]
                    strain[5, 3 * n + 2] = gradients[n, 0]
                    for i in range(3):
                        shape_rows[i, 3 * n + i] = shape_values[n]
                stiffness += strain.T @ elastic @ strain / 8.0
                mass_matrix += shape_rows.T @ shape_rows / 8.0
    return np.concatenate([stiffness, mass_matrix], 0)


def tent_valid(values, along):
    margin = FR - 1
    length = values.shape[along] - 2 * margin
    summed = None
    for offset in range(-margin, margin + 1):
        shifted = (FR - abs(offset)) * lax.slice_in_dim(
            values, margin + offset, margin + offset + length, axis=along
        )
        summed = shifted if summed is None else summed + shifted
    return summed


def tent_padded(values, along):
    margin = FR - 1
    widths = [(0, 0)] * values.ndim
    widths[along] = (margin, margin)
    return tent_valid(jnp.pad(values, widths), along)


def edge_weights(positions, count):
    summed = jnp.zeros(positions.shape, jnp.float32)
    for offset in range(-(FR - 1), FR):
        inside = (positions + offset >= 0) & (positions + offset < count)
        summed = summed + (FR - abs(offset)) * inside.astype(jnp.float32)
    return summed


def grid_positions(start, count):
    return start + jnp.arange(count, dtype=jnp.int32)


def span_block(x_start, x_count, y_start, y_count, total_x, total_rows, depth_count):
    first_weight = edge_weights(grid_positions(x_start, x_count), total_x)
    second_weight = edge_weights(grid_positions(y_start, y_count), total_rows)
    third_weight = edge_weights(grid_positions(0, depth_count), depth_count)
    return first_weight[:, None, None] * second_weight[None, :, None] * third_weight[None, None, :]


def inverse_block(x_start, x_count, y_start, y_count, total_x, total_rows, depth_count):
    first_index = grid_positions(x_start, x_count)
    second_index = grid_positions(y_start, y_count)
    spans = span_block(x_start, x_count, y_start, y_count, total_x, total_rows, depth_count)
    first_inside = ((first_index >= 0) & (first_index < total_x)).astype(jnp.float32)
    second_inside = ((second_index >= 0) & (second_index < total_rows)).astype(jnp.float32)
    inside = first_inside[:, None, None] * second_inside[None, :, None]
    return inside / jnp.maximum(spans, 1.0)


def update(design, sensitivity, measure, level):
    factor = jnp.sqrt(jnp.maximum(sensitivity, 0.0) / (jnp.exp(level) * measure))
    return jnp.clip(
        design * factor,
        jnp.maximum(design - MOVE_LIMIT, 0.0),
        jnp.minimum(design + MOVE_LIMIT, 1.0),
    )


def element_forms(node_values, tables):
    layer_count = node_values.shape[1] - 1
    row_count = node_values.shape[2]
    depth_count = node_values.shape[3]
    block_rows = 32
    padded = jnp.concatenate(
        [node_values, jnp.zeros((3, layer_count + 1, 1, depth_count), jnp.float32)], 2
    )
    lifted = jnp.concatenate(
        [padded[:, :, :, 1:], jnp.zeros((3, layer_count + 1, row_count + 1, 1), jnp.float32)], 3
    )

    def one_block(start):
        corners = []
        for a in (0, 1):
            for b in (0, 1):
                for c in (0, 1):
                    source = lifted if c else padded
                    corners.append(
                        lax.dynamic_slice(
                            source, (0, a, start + b, 0), (3, layer_count, block_rows, depth_count)
                        )
                    )
        stacked = jnp.stack(corners, 0).reshape(24, layer_count * block_rows * depth_count)
        product = jnp.dot(tables, stacked, precision=lax.Precision.HIGHEST)
        stiff_form = jnp.sum(product[:24] * stacked, 0).reshape(
            layer_count, block_rows, depth_count
        )
        mass_form = jnp.sum(product[24:] * stacked, 0).reshape(layer_count, block_rows, depth_count)
        return (stiff_form, mass_form)

    starts = jnp.arange(row_count // block_rows, dtype=jnp.int32) * block_rows
    stiff_blocks, mass_blocks = lax.map(one_block, starts)
    stiff_form = jnp.moveaxis(stiff_blocks, 0, 1).reshape(layer_count, row_count, depth_count)
    mass_form = jnp.moveaxis(mass_blocks, 0, 1).reshape(layer_count, row_count, depth_count)
    return (stiff_form, mass_form)


def local(design, mode_shapes, eigenvalues):
    margin = FR - 1
    slab_cells, own_rows, depth_count = design.shape
    total_x = slab_cells * lax.axis_size("slab")
    total_rows = own_rows * lax.axis_size("mode")
    x_start = lax.axis_index("slab") * slab_cells
    y_start = lax.axis_index("mode") * own_rows
    tables = jnp.asarray(element_tables(), jnp.float32)
    own_span = span_block(x_start, slab_cells, y_start, own_rows, total_x, total_rows, depth_count)
    extended = padded_2(design, (("slab", 0), ("mode", 1)), margin)
    own_density = tent_valid(tent_valid(tent_padded(extended, 2), 0), 1) / own_span
    density = lax.all_gather(own_density, "mode", axis=1, tiled=True)
    target = lax.psum(jnp.sum(own_density), ("slab", "mode"))
    plane = shifted_2(mode_shapes[:, :, 0], "slab", -1)
    node_values = jnp.concatenate([mode_shapes, plane[:, :, None]], 2)
    weights = jnp.exp(-KS_SHARP * eigenvalues)
    summed_weight = lax.psum(jnp.sum(weights), "mode")
    slope = PENALTY * (1.0 - FLOOR_MODULUS) * density * density

    def add_mode(number, partial_value):
        stiff_form, mass_form = element_forms(node_values[number], tables)
        return partial_value + weights[number] * (
            slope * stiff_form - eigenvalues[number] * mass_form
        )

    partial_value = lax.fori_loop(0, node_values.shape[0], add_mode, jnp.zeros_like(density))
    summed = lax.psum(partial_value, "mode")
    own_sum = lax.dynamic_slice_in_dim(summed, y_start, own_rows, 1)
    gradient = own_sum / summed_weight
    rim_values = padded_2(gradient / own_span, (("slab", 0), ("mode", 1)), margin)
    sensitivity = tent_valid(tent_valid(tent_padded(rim_values, 2), 0), 1)
    inverse = inverse_block(
        x_start - margin,
        slab_cells + 2 * margin,
        y_start - margin,
        own_rows + 2 * margin,
        total_x,
        total_rows,
        depth_count,
    )
    measure = tent_valid(tent_valid(tent_padded(inverse, 2), 0), 1)
    start_bounds = (jnp.asarray(LEVEL_LOW, jnp.float32), jnp.asarray(LEVEL_HIGH, jnp.float32))

    def bracket(count, bounds):
        lower, upper = bounds
        intervals = [(lower, upper)]
        middles = []
        for depth_step in range(4):
            following = []
            for bounds_pair in intervals:
                middle = (bounds_pair[0] + bounds_pair[1]) * 0.5
                middles.append(middle)
                following.append((bounds_pair[0], middle))
                following.append((middle, bounds_pair[1]))
            intervals = following
        candidates = jnp.stack(middles)
        partial_volumes = jnp.stack(
            [
                jnp.sum(update(design, sensitivity, measure, candidate) * measure)
                for candidate in middles
            ]
        )
        volumes = lax.psum(partial_volumes, ("slab", "mode"))
        heap_slot = jnp.asarray(0, jnp.int32)
        for depth_step in range(4):
            middle = candidates[heap_slot]
            above = volumes[heap_slot] > target
            lower = jnp.where(above, middle, lower)
            upper = jnp.where(above, upper, middle)
            heap_slot = 2 * heap_slot + 1 + above.astype(jnp.int32)
        return (lower, upper)

    lower, upper = lax.fori_loop(0, BISECT // 4, bracket, start_bounds)
    new_design = update(design, sensitivity, measure, (lower + upper) * 0.5)
    return (sensitivity, new_design)


def solution(mesh):
    in_specs = (P("slab", "mode", None), P("mode", None, "slab", None, None), P("mode"))
    out_specs = (P("slab", "mode", None), P("slab", "mode", None))
    return jax.shard_map(local, mesh=mesh, in_specs=in_specs, out_specs=out_specs, check_vma=False)
```

profile of v0, /device:TPU:0, one launch (start us, length us, event | category | flops | bytes accessed | tf_op | source)
XLA Modules:
  0.0 338.3 jit_solution(6758466817519506271)
XLA Ops:
  7.2 5.0 %collective-permute-start = (f32[2,32,128]{2,1,0:T(8,128)}, f32[2,32,128]{2,1,0:T(8,128)S(1)}, u32[]{:S(2)}, u32[]{:S(2)}) collective-permute-start(f32[2,32,128]{2,1,0:T(8,128)} %param.8), channel_id=1, source_target_pairs={{0,4},{4,8},{8,12},{12,16},{16,20},{20,24},{24,28},{1,5},{5,9},{9,... | collective-permute-start | bytes 98312 | tf_op jit(solution)/shard_map/ppermute | solution.py:27
  14.5 1.3 collective-permute-start.4
  19.5 1.3 collective-permute-start.3
  21.6 2.8 collective-permute-done.3
  25.3 6.5 %all_gather.3 = f32[2,128,128]{2,1,0:T(8,128)S(1)} all-gather(f32[2,32,128]{2,1,0:T(8,128)S(1)} %get-tuple-element.276), channel_id=1, replica_groups=mesh['slab'=8,'mode'=4] {'mode'}, dimensions={1}, use_global_device_ids=true | all-gather | bytes 163840 | tf_op jit(solution)/shard_map/all_gather | solution.py:188
  32.6 21.8 %while.39 = (s32[]{:T(128)}, f32[4,2,32,128]{3,2,1,0:T(8,128)S(1)}, f32[4,2,32,128]{3,2,1,0:T(8,128)S(1)}, s32[4]{0:T(128)S(1)}, f32[3,3,129,128]{3,2,1,0:T(8,12...) while((s32[]{:T(128)}, f32[4,2,32,128]{3,2,1,0:T(8,128)S(1)}, ...), condition=%wide.region_3.4_spmd.clone, body=%wide.region_0.3_spmd.sunk.clone.sunk | while | flops 114016264 | bytes 8065773 | solution.py:171
  36.3 1.4 fusion.78
  41.8 1.4 fusion.78
  47.2 1.4 fusion.78
  52.7 1.4 fusion.78
  55.4 8.0 %psum.32 = f32[]{:T(128)} all-reduce(f32[]{:T(128)} %bitcast.37), channel_id=1, replica_groups=mesh['slab'=8,'mode'=4] {'mode'}, use_global_device_ids=true, to_apply=%region_5.6 | all-reduce | flops 1 | bytes 8 | tf_op jit(solution)/shard_map/psum | solution.py:193
  63.4 26.3 %all-reduce.7.cloned.1.call-done = f32[2,128,128]{2,1,0:T(8,128)} async-done(((f32[2,128,128]{2,1,0:T(8,128)}), f32[2,128,128]{2,1,0:T(8,128)}) %all-reduce.7.cloned.1.call-update) | async-done | bytes 131088 | tf_op jit(solution)/shard_map/psum | solution.py:203
  89.7 1.5 fusion.32
  91.2 3.4 collective-permute-start.5
  94.6 1.3 collective-permute-start.6
  96.2 4.2 %collective-permute-done.6 = f32[2,32,128]{2,1,0:T(8,128)S(1)} collective-permute-done((f32[2,32,128]{2,1,0:T(8,128)S(1)}, f32[2,32,128]{2,1,0:T(8,128)S(1)}, u32[]{:S(2)}, u32[]{:S(2)}) %collective-permute-start.6) | collective-permute-done | bytes 32800 | tf_op jit(solution)/shard_map/ppermute | solution.py:28
  103.0 43.4 %psum.33 = f32[]{:T(128)} all-reduce(f32[]{:T(128)} %get-tuple-element.275), channel_id=1, replica_groups=mesh['slab'=8,'mode'=4] {'slab','mode'}, use_global_device_ids=true, to_apply=%region_7.0 | all-reduce | flops 1 | bytes 8 | tf_op jit(solution)/shard_map/psum | solution.py:189
  146.7 183.9 %while.38 = (s32[]{:T(128)}, f32[]{:T(128)}, f32[]{:T(128)}, f32[2,32,128]{2,1,0:T(8,128)S(1)}, f32[2,32,128]{2,1,0:T(8,128)S(1)}, /*index=5*/f32[2,32,128]{2,1,...) while((s32[]{:T(128)}, f32[]{:T(128)}, f32[]{:T(128)}, ...), condition=%wide.region_25.26_spmd, body=%wide.region_8.25_spmd.sunk | while | flops 901183 | bytes 99802 | solution.py:249
  148.4 9.3 %stack.266 = f32[15]{0:T(128)S(1)} concatenate(f32[1]{0:T(128)} %bitcast.128, f32[1]{0:T(128)} %bitcast.129, f32[1]{0:T(128)} %bitcast.130, f32[1]{0:T(128)} %bitcast.131, f32[1]{0:T(128)} %bitcast.132, f32[1]{0:T(128)} %bitcast.133, f32[1]{0:T(128)} %bitcast.134, f32[1]{0:T(128)} %bitcast.135, f32[1]{0:T(128)} %bitcast.136, f32[1]{0:T(128)} %bitcast.137, f32[1]{0:T(128)} %bitcast.138, ...), dimensions={0} | concatenate | bytes 120 | tf_op jit(solution)/shard_map/while/body/eval_jaxpr/stack | solution.py:233
  157.8 39.3 %psum.35 = f32[15]{0:T(128)S(1)} all-reduce(f32[15]{0:T(128)S(1)} %stack.266), channel_id=1, replica_groups=mesh['slab'=8,'mode'=4] {'slab','mode'}, use_global_device_ids=true, to_apply=%region_24.24 | all-reduce | flops 15 | bytes 120 | tf_op jit(solution)/shard_map/while/body/eval_jaxpr/psum | solution.py:239
  209.2 9.3 %stack.266 = f32[15]{0:T(128)S(1)} concatenate(f32[1]{0:T(128)} %bitcast.128, f32[1]{0:T(128)} %bitcast.129, f32[1]{0:T(128)} %bitcast.130, f32[1]{0:T(128)} %bitcast.131, f32[1]{0:T(128)} %bitcast.132, f32[1]{0:T(128)} %bitcast.133, f32[1]{0:T(128)} %bitcast.134, f32[1]{0:T(128)} %bitcast.135, f32[1]{0:T(128)} %bitcast.136, f32[1]{0:T(128)} %bitcast.137, f32[1]{0:T(128)} %bitcast.138, ...), dimensions={0} | concatenate | bytes 120 | tf_op jit(solution)/shard_map/while/body/eval_jaxpr/stack | solution.py:233
  218.5 41.0 %psum.35 = f32[15]{0:T(128)S(1)} all-reduce(f32[15]{0:T(128)S(1)} %stack.266), channel_id=1, replica_groups=mesh['slab'=8,'mode'=4] {'slab','mode'}, use_global_device_ids=true, to_apply=%region_24.24 | all-reduce | flops 15 | bytes 120 | tf_op jit(solution)/shard_map/while/body/eval_jaxpr/psum | solution.py:239
  271.7 9.3 %stack.266 = f32[15]{0:T(128)S(1)} concatenate(f32[1]{0:T(128)} %bitcast.128, f32[1]{0:T(128)} %bitcast.129, f32[1]{0:T(128)} %bitcast.130, f32[1]{0:T(128)} %bitcast.131, f32[1]{0:T(128)} %bitcast.132, f32[1]{0:T(128)} %bitcast.133, f32[1]{0:T(128)} %bitcast.134, f32[1]{0:T(128)} %bitcast.135, f32[1]{0:T(128)} %bitcast.136, f32[1]{0:T(128)} %bitcast.137, f32[1]{0:T(128)} %bitcast.138, ...), dimensions={0} | concatenate | bytes 120 | tf_op jit(solution)/shard_map/while/body/eval_jaxpr/stack | solution.py:233
  281.0 39.1 %psum.35 = f32[15]{0:T(128)S(1)} all-reduce(f32[15]{0:T(128)S(1)} %stack.266), channel_id=1, replica_groups=mesh['slab'=8,'mode'=4] {'slab','mode'}, use_global_device_ids=true, to_apply=%region_24.24 | all-reduce | flops 15 | bytes 120 | tf_op jit(solution)/shard_map/while/body/eval_jaxpr/psum | solution.py:239
  (126 shorter events, 27.5 us)
Async XLA Ops:
  7.2 24.6 %copy-start = (f32[1,3,2,128,128]{4,3,2,1,0:T(8,128)S(1)}, f32[1,3,2,128,128]{4,3,2,1,0:T(8,128)}, u32[]{:S(2)}) copy-start(f32[1,3,2,128,128]{4,3,2,1,0:T(8,128)} %param.9) | copy-start | bytes 1179652
  7.2 82.5 %all-reduce.7.cloned.1.call-start = ((), (), s32[]{:S(2)}) async-start(), calls=%async_computation | async-start | bytes 262144 | tf_op jit(solution)/shard_map/psum | solution.py:203
  7.2 8.9 %collective-permute-start = (f32[2,32,128]{2,1,0:T(8,128)}, f32[2,32,128]{2,1,0:T(8,128)S(1)}, u32[]{:S(2)}, u32[]{:S(2)}) collective-permute-start(f32[2,32,128]{2,1,0:T(8,128)} %param.8), channel_id=1, source_target_pairs={{0,4},{4,8},{8,12},{12,16},{16,20},{20,24},{24,28},{1,5},{5,9},{9,... | collective-permute-start | bytes 98312 | tf_op jit(solution)/shard_map/ppermute | solution.py:27
  12.2 6.0 %collective-permute-start.1 = (f32[2,32,128]{2,1,0:T(8,128)}, f32[2,32,128]{2,1,0:T(8,128)S(1)}, u32[]{:S(2)}, u32[]{:S(2)}) collective-permute-start(f32[2,32,128]{2,1,0:T(8,128)} %param.8), channel_id=1, source_target_pairs={{4,0},{8,4},{12,8},{16,12},{20,16},{24,20},{28,24},{5,1},{9,5},{13... | collective-permute-start | bytes 98312 | tf_op jit(solution)/shard_map/ppermute | solution.py:28
  14.5 17.3 %collective-permute-start.4 = (f32[1,3,128,128]{3,2,1,0:T(8,128)S(1)}, f32[1,3,128,128]{3,2,1,0:T(8,128)S(1)}, u32[]{:S(2)}, u32[]{:S(2)}) collective-permute-start(f32[1,3,128,128]{3,2,1,0:T(8,128)S(1)} %slice_bitcast_fusion), channel_id=1, source_target_pairs={{4,0},{8,4},{12,8},{16,12},{20,16},{24,20},{28,24},{5,1},{9,5},{13... | collective-permute-start | bytes 589832 | tf_op jit(solution)/shard_map/ppermute | solution.py:36
  18.2 3.3 collective-permute-start.2
  19.5 4.8 %collective-permute-start.3 = (f32[6,2,128]{2,1,0:T(2,128)S(1)}, f32[6,2,128]{2,1,0:T(2,128)S(1)}, u32[]{:S(2)}, u32[]{:S(2)}) collective-permute-start(f32[6,2,128]{2,1,0:T(2,128)S(1)} %get-tuple-element.285), channel_id=1, source_target_pairs={{1,0},{2,1},{3,2},{5,4},{6,5},{7,6},{9,8},{10,9},{11,10},{13,12},{... | collective-permute-start | bytes 18440 | tf_op jit(solution)/shard_map/ppermute | solution.py:28
  31.8 0.7 copy-start.1
  54.4 92.3 %copy-start.2 = (f32[2,32,128]{2,1,0:T(8,128)S(1)}, f32[2,32,128]{2,1,0:T(8,128)}, u32[]{:S(2)}) copy-start(f32[2,32,128]{2,1,0:T(8,128)} %param.8) | copy-start | bytes 98308
  91.2 5.0 %collective-permute-start.5 = (f32[2,32,128]{2,1,0:T(8,128)S(1)}, f32[2,32,128]{2,1,0:T(8,128)S(1)}, u32[]{:S(2)}, u32[]{:S(2)}) collective-permute-start(f32[2,32,128]{2,1,0:T(8,128)S(1)} %fusion.32), channel_id=1, source_target_pairs={{0,4},{4,8},{8,12},{12,16},{16,20},{20,24},{24,28},{1,5},{5,9},{9,... | collective-permute-start | bytes 98312 | tf_op jit(solution)/shard_map/ppermute | solution.py:27
  94.6 5.8 %collective-permute-start.6 = (f32[2,32,128]{2,1,0:T(8,128)S(1)}, f32[2,32,128]{2,1,0:T(8,128)S(1)}, u32[]{:S(2)}, u32[]{:S(2)}) collective-permute-start(f32[2,32,128]{2,1,0:T(8,128)S(1)} %fusion.32), channel_id=1, source_target_pairs={{4,0},{8,4},{12,8},{16,12},{20,16},{24,20},{28,24},{5,1},{9,5},{13... | collective-permute-start | bytes 98312 | tf_op jit(solution)/shard_map/ppermute | solution.py:28
  100.4 46.1 %collective-permute-start.7 = (f32[6,2,128]{2,1,0:T(2,128)S(1)}, f32[6,2,128]{2,1,0:T(2,128)S(1)}, u32[]{:S(2)}, u32[]{:S(2)}) collective-permute-start(f32[6,2,128]{2,1,0:T(2,128)S(1)} %get-tuple-element.282), channel_id=1, source_target_pairs={{0,1},{1,2},{2,3},{4,5},{5,6},{6,7},{8,9},{9,10},{10,11},{12,13},{... | collective-permute-start | bytes 18440 | tf_op jit(solution)/shard_map/ppermute | solution.py:27
  101.7 44.8 %collective-permute-start.8 = (f32[6,2,128]{2,1,0:T(2,128)S(1)}, f32[6,2,128]{2,1,0:T(2,128)S(1)}, u32[]{:S(2)}, u32[]{:S(2)}) collective-permute-start(f32[6,2,128]{2,1,0:T(2,128)S(1)} %get-tuple-element.283), channel_id=1, source_target_pairs={{1,0},{2,1},{3,2},{5,4},{6,5},{7,6},{9,8},{10,9},{11,10},{13,12},{... | collective-permute-start | bytes 18440 | tf_op jit(solution)/shard_map/ppermute | solution.py:28
  330.7 0.7 copy-start.3
Sparse Core Ops, SparseCore 0:
  55.3 34.3 all-reduce.6
where the time goes:
time: 340 us; the launch traced here: 338 us
  blocking collectives  177 us (52%)
  local copies, waits for them, and re-layouts  41.6 us (12%)
  loops' own time  37.9 us (11%)
  waiting for transfers between devices  34.9 us (10%)
  starting transfers between devices  17.4 us (5%)
  between operations  15.1 us (4%)
  other arithmetic  8.61 us (3%)
  matrix products  5.46 us (2%)
    psum x3, blocking collectives, bracket(): volumes = lax.psum(partial_volumes, ('slab', 'mode'))  119 us
    psum x1, blocking collectives, local(): target = lax.psum(jnp.sum(own_density), ('slab', 'mode'))  43.4 us
    another operation x3, local copies, waits for them, and re-layouts, bracket(): jnp.stack([jnp.sum(update(design, sensitivity, measure, candidate) * meas...  27.9 us
    psum x1, waiting for transfers between devices, local(): summed = lax.psum(partial_value, 'mode')  26.3 us
    another operation x1, loops' own time, local(): lower, upper = lax.fori_loop(0, BISECT // 4, bracket, start_bounds)  26.2 us
    another operation x1, loops' own time, element_forms(): stiff_blocks, mass_blocks = lax.map(one_block, starts)  11.6 us
    ppermute x4, starting transfers between devices, padded_2(): before = lax.ppermute(last, axis, up)  10.9 us
    ppermute x4, waiting for transfers between devices, padded_2(): after = lax.ppermute(leading, axis, down)  8.31 us
  transfers between devices with their start and end apart: 10, of which 5 were waited for; matrix products, arithmetic and copies ran while one was open for 1% of the time, Pallas kernels for 0%

commit v1 on v0

v1 whole, which is shorter than its diff:
```python
import functools
import math

import jax
import jax.numpy as jnp
from jax import lax
from jax.experimental import pallas as pl
from jax.experimental.pallas import tpu as pltpu
from jax.sharding import PartitionSpec as P

FR = 3
BISECT = 12
KS_SHARP = 2.0
PENALTY = 3.0
FLOOR_MODULUS = 0.001
MOVE_LIMIT = 0.2
POISSON = 0.3
LEVEL_LOW = -14.0
LEVEL_HIGH = 14.0

MARGIN = FR - 1
PAD = 8
STEPS = BISECT // 2
TRIALS = 2**STEPS
LAME = POISSON / ((1.0 + POISSON) * (1.0 - 2.0 * POISSON))
SHEAR = 0.5 / (1.0 + POISSON)
MESH = pl.DeviceIdType.MESH
DIRECTIONS = [(dx, dy) for dx in (-1, 0, 1) for dy in (-1, 0, 1) if (dx, dy) != (0, 0)]


def edge_weight(position, count):
    total = jnp.zeros(position.shape, jnp.float32)
    for offset in range(-MARGIN, MARGIN + 1):
        inside = (position + offset >= 0) & (position + offset < count)
        total = total + jnp.where(inside, float(FR - abs(offset)), 0.0)
    return total


def axis_tables(position, count):
    measure = jnp.zeros(position.shape, jnp.float32)
    for offset in range(-MARGIN, MARGIN + 1):
        moved = position + offset
        inside = (moved >= 0) & (moved < count)
        weight = jnp.maximum(edge_weight(moved, count), 1.0)
        measure = measure + jnp.where(inside, float(FR - abs(offset)) / weight, 0.0)
    return edge_weight(position, count), measure


def filtered(ext, cells, rows, depth):
    lane = lax.broadcasted_iota(jnp.int32, (rows, depth), 1)
    results = []
    for cell in range(cells):
        along = None
        for offset in range(2 * MARGIN + 1):
            term = float(FR - abs(offset - MARGIN)) * ext[cell + offset]
            along = term if along is None else along + term
        total = None
        for offset in range(-MARGIN, MARGIN + 1):
            moved = pltpu.roll(along, (-offset) % (rows + 2 * PAD), 0) if offset else along
            term = float(FR - abs(offset)) * moved[PAD : PAD + rows]
            total = term if total is None else total + term
        value = float(FR) * total
        for offset in range(1, MARGIN + 1):
            after = jnp.where(lane < depth - offset, pltpu.roll(total, depth - offset, 1), 0.0)
            before = jnp.where(lane >= offset, pltpu.roll(total, offset, 1), 0.0)
            value = value + float(FR - offset) * (after + before)
        results.append(value)
    return results


def plane_parts(view, row, sub, node_rows, depth):
    after = row + sub
    following = view(pl.multiple_of(jnp.minimum(after, node_rows - 8), 8), 8)
    following = jnp.where(after < node_rows, following, jnp.zeros_like(following))
    value = jnp.concatenate([view(row, sub), following], 0)
    lane = lax.broadcasted_iota(jnp.int32, value.shape, 1)
    lifted = jnp.where(lane < depth - 1, pltpu.roll(value, depth - 1, 1), 0.0)
    parts = {}
    for z, base in ((0, value + lifted), (1, lifted - value)):
        above = pltpu.roll(base, sub + 7, 0)[:sub]
        parts[0, z] = base[:sub] + above
        parts[1, z] = above - base[:sub]
    return parts


def total_of(terms):
    result = terms[0]
    for term in terms[1:]:
        result = result + term
    return result


def energies(first, second):
    h = []
    for a, b in zip(first, second):
        h.append({(p, *key): (b[key] - a[key] if p else a[key] + b[key]) for p in (0, 1) for key in a})
    u, v, w = h
    sq = lambda value: value * value
    squares = [{key: sq(value) for key, value in comp.items()} for comp in h]
    su, sv, sw = squares
    q1 = su[1, 0, 0] + sv[0, 1, 0] + sw[0, 0, 1]
    q2 = total_of([su[1, 1, 0], su[1, 0, 1], sv[1, 1, 0], sv[0, 1, 1], sw[1, 0, 1], sw[0, 1, 1]])
    q3 = su[1, 1, 1] + sv[1, 1, 1] + sw[1, 1, 1]
    m0 = su[0, 0, 0] + sv[0, 0, 0] + sw[0, 0, 0]
    m1 = q1 + total_of([su[0, 1, 0], su[0, 0, 1], sv[1, 0, 0], sv[0, 0, 1], sw[1, 0, 0], sw[0, 1, 0]])
    m2 = q2 + total_of([su[0, 1, 1], sv[1, 0, 1], sw[1, 1, 0]])
    div0 = sq(u[1, 0, 0] + v[0, 1, 0] + w[0, 0, 1])
    div1 = sq(v[1, 1, 0] + w[1, 0, 1]) + sq(u[1, 1, 0] + w[0, 1, 1]) + sq(u[1, 0, 1] + v[0, 1, 1])
    cut0 = sq(u[0, 1, 0] + v[1, 0, 0]) + sq(u[0, 0, 1] + w[1, 0, 0]) + sq(v[0, 0, 1] + w[0, 1, 0])
    cut1 = sq(u[0, 1, 1] + v[1, 0, 1]) + sq(u[0, 1, 1] + w[1, 1, 0]) + sq(v[1, 0, 1] + w[1, 1, 0])
    stiff = (
        (LAME / 16.0) * div0
        + (SHEAR / 16.0) * (2.0 * q1 + cut0)
        + (LAME / 48.0) * div1
        + (SHEAR / 48.0) * (3.0 * q2 + cut1)
        + ((LAME + 4.0 * SHEAR) / 144.0) * q3
    )
    mass = (1.0 / 64.0) * m0 + (1.0 / 192.0) * m1 + (1.0 / 576.0) * m2 + (1.0 / 1728.0) * q3
    return stiff, mass


def kernel(
    slabs, groups,
    design_ref, shapes_ref, eig_ref, sens_ref, new_ref,
    design_ext, grad_ext, plane, outgoing, incoming, weight_tiles, partial, row_tiles, column_tiles, trial_rows,
    design_sems, grad_sems, plane_sems, form_sems, weight_sems, row_sems, column_sems,
):
    cells, rows, depth = design_ref.shape
    modes, node_rows = shapes_ref.shape[0], shapes_ref.shape[3]
    total_x, total_rows = cells * slabs, rows * groups
    s, m = lax.axis_index("slab"), lax.axis_index("mode")
    sub = 16 if rows % 16 == 0 else 8

    design_ext[...] = jnp.zeros_like(design_ext)
    grad_ext[...] = jnp.zeros_like(grad_ext)

    @pl.when(s == slabs - 1)
    def _():
        plane[...] = jnp.zeros_like(plane)

    barrier = pltpu.get_barrier_semaphore()
    expected = (groups - 1) + (slabs - 1)
    for d in range(1, groups):
        pl.semaphore_signal(barrier, inc=1, device_id=(s, lax.rem(m + d, groups)), device_id_type=MESH)
    for d in range(1, slabs):
        pl.semaphore_signal(barrier, inc=1, device_id=(lax.rem(s + d, slabs), m), device_id_type=MESH)
    for dx, dy in DIRECTIONS:
        if dx and dy:
            fits = (s + dx >= 0) & (s + dx < slabs) & (m + dy >= 0) & (m + dy < groups)
            expected = expected + fits.astype(jnp.int32)

            @pl.when(fits)
            def _():
                pl.semaphore_signal(barrier, inc=1, device_id=(s + dx, m + dy), device_id_type=MESH)

    pl.semaphore_wait(barrier, expected)

    def plane_copy():
        return pltpu.make_async_remote_copy(
            src_ref=shapes_ref.at[:, :, 0], dst_ref=plane,
            send_sem=plane_sems.at[0], recv_sem=plane_sems.at[1],
            device_id=(s - 1, m), device_id_type=MESH,
        )

    @pl.when(s > 0)
    def _():
        plane_copy().start()

    def halo(source, x_off, y_off, target, sems, number):
        dx, dy = DIRECTIONS[number]
        x_from, x_count, x_to = {
            1: (cells - MARGIN, MARGIN, 0), -1: (0, MARGIN, MARGIN + cells), 0: (0, cells, MARGIN)}[dx]
        y_from, y_count, y_to = {
            1: (rows - PAD, PAD, 0), -1: (0, PAD, PAD + rows), 0: (0, rows, PAD)}[dy]
        return pltpu.make_async_remote_copy(
            src_ref=source.at[pl.ds(x_off + x_from, x_count), pl.ds(y_off + y_from, y_count)],
            dst_ref=target.at[pl.ds(x_to, x_count), pl.ds(y_to, y_count)],
            send_sem=sems.at[0, number], recv_sem=sems.at[1, number],
            device_id=(s + dx, m + dy), device_id_type=MESH,
        )

    def each_halo(source, x_off, y_off, target, sems, action, sign):
        for number, (dx, dy) in enumerate(DIRECTIONS):
            x, y = s + sign * dx, m + sign * dy

            @pl.when((x >= 0) & (x < slabs) & (y >= 0) & (y < groups))
            def _():
                getattr(halo(source, x_off, y_off, target, sems, number), action)()

    design_halo = functools.partial(each_halo, design_ref, 0, 0, design_ext, design_sems)
    grad_halo = functools.partial(each_halo, grad_ext, MARGIN, PAD, grad_ext, grad_sems)

    weights = [jnp.exp(-KS_SHARP * jnp.full((8, depth), eig_ref[k])) for k in range(modes)]
    weight_tiles[m] = total_of(weights)

    def mode_exchange(buffer, sems):
        return [
            pltpu.make_async_remote_copy(
                src_ref=buffer.at[m], dst_ref=buffer.at[m],
                send_sem=sems.at[0, d], recv_sem=sems.at[1, d],
                device_id=(s, lax.rem(m + d, groups)), device_id_type=MESH,
            )
            for d in range(1, groups)
        ]

    def slab_exchange(buffer, sems):
        return [
            pltpu.make_async_remote_copy(
                src_ref=buffer.at[s], dst_ref=buffer.at[s],
                send_sem=sems.at[0, d], recv_sem=sems.at[1, d],
                device_id=(lax.rem(s + d, slabs), m), device_id_type=MESH,
            )
            for d in range(1, slabs)
        ]

    weight_copies = mode_exchange(weight_tiles, weight_sems)
    for copy in weight_copies:
        copy.start()
    design_halo("start", 1)

    def node_view(mode, comp, layer):
        if layer == cells:
            return lambda row, count: plane[mode, comp, pl.ds(row, count), :]
        return lambda row, count: shapes_ref[mode, comp, layer, pl.ds(row, count), :]

    def layer_forms(layer, group):
        def step(number, carry):
            row = pl.multiple_of(group * rows + number * sub, 8)
            stiff_sum = mass_sum = None
            for mode in range(modes):
                first, second = [
                    [plane_parts(node_view(mode, comp, at), row, sub, node_rows, depth) for comp in range(3)]
                    for at in (layer, layer + 1)
                ]
                stiff, mass = energies(first, second)
                weight = weights[mode][0:1]
                stiff = weight * stiff
                mass = (weight * eig_ref[mode]) * mass
                stiff_sum = stiff if mode == 0 else stiff_sum + stiff
                mass_sum = mass if mode == 0 else mass_sum + mass
            at = pl.multiple_of(number * sub, 8)
            outgoing[group, layer, 0, pl.ds(at, sub), :] = stiff_sum
            outgoing[group, layer, 1, pl.ds(at, sub), :] = mass_sum
            return carry

        lax.fori_loop(0, rows // sub, step, 0)

    def form_copy(layer, d):
        group = lax.rem(m + d, groups)
        return pltpu.make_async_remote_copy(
            src_ref=outgoing.at[group, layer], dst_ref=incoming.at[d, layer],
            send_sem=form_sems.at[0, layer, d], recv_sem=form_sems.at[1, layer, d],
            device_id=(s, group), device_id_type=MESH,
        )

    order = list(range(1, groups)) + [0]
    for layer in range(cells):
        if layer == cells - 1:
            design_ext[MARGIN : MARGIN + cells, PAD : PAD + rows, :] = design_ref[...]
            x_tables = [axis_tables(jnp.full((1, depth), s * cells + i, jnp.int32), total_x) for i in range(cells)]
            y_tables = axis_tables(m * rows + lax.broadcasted_iota(jnp.int32, (rows, depth), 0), total_rows)
            z_tables = axis_tables(lax.broadcasted_iota(jnp.int32, (1, depth), 1), depth)
            spans = [x[0] * (y_tables[0] * z_tables[0]) for x in x_tables]
            measures = [x[1] * (y_tables[1] * z_tables[1]) for x in x_tables]
            design_halo("wait_recv", -1)
            densities = [f / span for f, span in zip(filtered(design_ext, cells, rows, depth), spans)]

            @pl.when(s < slabs - 1)
            def _():
                plane_copy().wait_recv()

        for d in order:
            layer_forms(layer, lax.rem(m + d, groups))
            if d:
                form_copy(layer, d).start()

    for copy in weight_copies:
        copy.wait_recv()
    weight_total = total_of([weight_tiles[i] for i in range(groups)])[0:1]
    for cell in range(cells):
        stiff, mass = outgoing[m, cell, 0], outgoing[m, cell, 1]
        for d in range(1, groups):
            form_copy(cell, d).wait_recv()
            stiff = stiff + incoming[d, cell, 0]
            mass = mass + incoming[d, cell, 1]
        slope = PENALTY * (1.0 - FLOOR_MODULUS) * densities[cell] * densities[cell]
        gradient = (slope * stiff - mass) / weight_total
        grad_ext[MARGIN + cell, PAD : PAD + rows, :] = gradient / spans[cell]
    grad_halo("start", 1)
    grad_halo("wait_recv", -1)
    sensitivities = filtered(grad_ext, cells, rows, depth)

    lowers, uppers, scales = [], [], []
    for cell in range(cells):
        sensitivity, measure = sensitivities[cell], measures[cell]
        sens_ref[cell] = sensitivity
        design = design_ref[cell]
        scales.append(design * jnp.sqrt(jnp.maximum(sensitivity, 0.0) / measure) * measure)
        lowers.append(jnp.maximum(design - MOVE_LIMIT, 0.0) * measure)
        uppers.append(jnp.minimum(design + MOVE_LIMIT, 1.0) * measure)
    lower, upper, scale = [jnp.concatenate(parts, 0) for parts in (lowers, uppers, scales)]
    trial_rows[1] = lower
    trial_rows[2] = upper

    def folded(value):
        return jnp.sum(value, axis=0, keepdims=True)

    lane = lax.broadcasted_iota(jnp.int32, (8, depth), 1)
    low = jnp.full((1, 1), LEVEL_LOW, jnp.float32)
    target = None
    width = LEVEL_HIGH - LEVEL_LOW
    copies = []
    for turn in range(2):
        width = width / TRIALS
        trial_rows[0] = scale * jnp.exp(-0.5 * low)
        for trial in range(0, TRIALS, 8):
            lines = []
            for number in range(trial, trial + 8):
                if number == 0:
                    lines.append(folded(total_of(densities)))
                    continue
                factor = math.exp(-0.5 * width * number)
                lines.append(folded(jnp.minimum(jnp.maximum(trial_rows[0] * factor, trial_rows[1]), trial_rows[2])))
            partial[trial : trial + 8, :] = jnp.concatenate(lines, 0)
        if turn == 0:
            partial[TRIALS:, :] = jnp.zeros((partial.shape[0] - TRIALS, depth), jnp.float32)
        row_tiles[turn, m] = lax.dot_general(
            jnp.ones((8, depth), jnp.float32), partial[...], (((1,), (1,)), ((), ())),
            precision=lax.Precision.HIGHEST, preferred_element_type=jnp.float32,
        )
        across = mode_exchange(row_tiles.at[turn], row_sems.at[turn])
        for copy in across:
            copy.start()
        for copy in across:
            copy.wait_recv()
        column_tiles[turn, s] = total_of([row_tiles[turn, i] for i in range(groups)])
        along = slab_exchange(column_tiles.at[turn], column_sems.at[turn])
        for copy in along:
            copy.start()
        for copy in along:
            copy.wait_recv()
        copies += across + along
        volumes = total_of([column_tiles[turn, i] for i in range(slabs)])
        if turn == 0:
            target = volumes[:, 0:1]
        above = (volumes > target) & (lane >= 1) & (lane < TRIALS)
        count = jnp.sum(jnp.where(above, 1.0, 0.0), axis=1, keepdims=True)
        low = low + count[0:1] * width
    shrink = jnp.exp(-0.5 * (low + 0.5 * width))
    for cell in range(cells):
        design = design_ref[cell]
        factor = jnp.sqrt(jnp.maximum(sensitivities[cell], 0.0) / measures[cell]) * shrink
        new_ref[cell] = jnp.minimum(
            jnp.maximum(design * factor, jnp.maximum(design - MOVE_LIMIT, 0.0)),
            jnp.minimum(design + MOVE_LIMIT, 1.0),
        )

    @pl.when(s > 0)
    def _():
        plane_copy().wait_send()

    for copy in copies + weight_copies:
        copy.wait_send()
    for layer in range(cells):
        for d in range(1, groups):
            form_copy(layer, d).wait_send()
    design_halo("wait_send", 1)
    grad_halo("wait_send", 1)


def local(slabs, groups, design, mode_shapes, eigenvalues):
    cells, rows, depth = design.shape
    modes, node_rows = mode_shapes.shape[0], mode_shapes.shape[3]
    f32 = jnp.float32
    ext = pltpu.VMEM((cells + 2 * MARGIN, rows + 2 * PAD, depth), f32)
    forms = pltpu.VMEM((groups, cells, 2, rows, depth), f32)
    dma = pltpu.SemaphoreType.DMA
    vmem = pl.BlockSpec(memory_space=pltpu.VMEM)
    return pl.pallas_call(
        functools.partial(kernel, slabs, groups),
        out_shape=[jax.ShapeDtypeStruct(design.shape, f32)] * 2,
        in_specs=[vmem, vmem, pl.BlockSpec(memory_space=pltpu.SMEM)],
        out_specs=[vmem, vmem],
        scratch_shapes=[
            ext, ext,
            pltpu.VMEM((modes, 3, node_rows, depth), f32),
            forms, forms,
            pltpu.VMEM((groups, 8, depth), f32),
            pltpu.VMEM((128, depth), f32),
            pltpu.VMEM((2, groups, 8, 128), f32),
            pltpu.VMEM((2, slabs, 8, 128), f32),
            pltpu.VMEM((3, cells * rows, depth), f32),
            dma((2, len(DIRECTIONS))), dma((2, len(DIRECTIONS))), dma((2,)),
            dma((2, cells, groups)), dma((2, groups)), dma((2, 2, groups)), dma((2, 2, slabs)),
        ],
        compiler_params=pltpu.CompilerParams(
            collective_id=0, has_side_effects=True, vmem_limit_bytes=32 * 1024 * 1024
        ),
    )(design, mode_shapes, eigenvalues)


def solution(mesh):
    in_specs = (P("slab", "mode", None), P("mode", None, "slab", None, None), P("mode"))
    out_specs = (P("slab", "mode", None), P("slab", "mode", None))
    body = functools.partial(local, mesh.shape["slab"], mesh.shape["mode"])
    return jax.shard_map(body, mesh=mesh, in_specs=in_specs, out_specs=out_specs, check_vma=False)
```

time: 340 us -> 41 us (0.12)
  blocking collectives: 177 us -> 0 us
  local copies, waits for them, and re-layouts: 41.6 us -> 2.98 us
  loops' own time: 37.9 us -> 0 us
  Pallas kernels: 0 us -> 36.5 us
  waiting for transfers between devices: 34.9 us -> 0 us
  starting transfers between devices: 17.4 us -> 0 us
  between operations: 15.1 us -> 1.29 us
  other arithmetic: 8.61 us -> 0 us
  matrix products: 5.46 us -> 0 us
    psum x5 -> x0, blocking collectives: 171 us -> none  [the longest x3 119 us: bracket(): volumes = lax.psum(partial_volumes, ('slab', 'mode'))]
    another operation x2 -> x0, loops' own time: 37.9 us -> none  [the longest x1 26.2 us: local(): lower, upper = lax.fori_loop(0, BISECT // 4, bracket, start_bounds)]
    pallas_call x0 -> x1, Pallas kernels: none -> 36.5 us  [local(): pl.pallas_call(functools.partial(kernel, slabs, groups), out_shape=[jax.S...]
    another operation x10 -> x0, local copies, waits for them, and re-layouts: 28.3 us -> none  [the longest x3 27.9 us: bracket(): jnp.stack([jnp.sum(update(design, sensitivity, measure, candidate) * meas...]
    psum x1 -> x0, waiting for transfers between devices: 26.3 us -> none  [local(): summed = lax.psum(partial_value, 'mode')]
    ppermute x9 -> x0, starting transfers between devices: 17.4 us -> none  [the longest x4 10.9 us: padded_2(): before = lax.ppermute(last, axis, up)]
    dynamic_slice x16 -> x0, local copies, waits for them, and re-layouts: 9.62 us -> none  [the longest x9 5.34 us: bracket(): above = volumes[heap_slot] > target]
    ppermute x9 -> x0, waiting for transfers between devices: 8.58 us -> none  [the longest x4 8.31 us: padded_2(): after = lax.ppermute(leading, axis, down)]
  transfers between devices with their start and end apart: 10 -> 0, of which waited for: 5 -> 0; matrix products, arithmetic and copies ran while one was open for 1% -> 0% of each run, Pallas kernels for 0% -> 0%
where the time goes in v1:
time: 41 us; the launch traced here: 40.8 us
  Pallas kernels  36.5 us (89%)
  local copies, waits for them, and re-layouts  2.98 us (7%)
  between operations  1.29 us (3%)
    pallas_call x1, Pallas kernels, local(): pl.pallas_call(functools.partial(kernel, slabs, groups), out_shape=[jax.S...  36.5 us
    unnamed x6, local copies, waits for them, and re-layouts  2.98 us

profile of v1, /device:TPU:0, one launch (start us, length us, event | category | flops | bytes accessed | tf_op | source)
XLA Modules:
  0.0 40.8 jit_solution(6830467470123494927)
XLA Ops:
  1.3 0.0 copy-start
  1.3 1.0 %copy-done = f32[1,3,2,128,128]{4,3,2,1,0:T(8,128)S(1)} copy-done((f32[1,3,2,128,128]{4,3,2,1,0:T(8,128)S(1)}, f32[1,3,2,128,128]{4,3,2,1,0:T(8,128)}, u32[]{:S(2)}) %copy-start) | copy-done | bytes 393240
  2.3 0.0 copy-start.1
  2.3 0.8 %copy-done.1 = f32[2,32,128]{2,1,0:T(8,128)S(1)} copy-done((f32[2,32,128]{2,1,0:T(8,128)S(1)}, f32[2,32,128]{2,1,0:T(8,128)}, u32[]{:S(2)}) %copy-start.1) | copy-done | bytes 32792
  3.0 36.5 %shard_map.50 = (f32[2,32,128]{2,1,0:T(8,128)S(1)}, f32[2,32,128]{2,1,0:T(8,128)S(1)}) custom-call(f32[2,32,128]{2,1,0:T(8,128)S(1)} %copy-done.1, f32[1,3,2,128,128]{4,3,2,1,0:T(8,128)S(1)} %copy-done, f32[1]{0:T(128)S(6)} %copy.7.eig_ref), custom_call_target="tpu_custom_call" | custom-call | tf_op jit(solution)/shard_map/pallas_call | solution.py:379
  39.6 0.6 %copy.8 = f32[2,32,128]{2,1,0:T(8,128)} copy(f32[2,32,128]{2,1,0:T(8,128)S(1)} %get-tuple-element.4) | data formatting | bytes 65536
  40.2 0.6 %copy.9 = f32[2,32,128]{2,1,0:T(8,128)} copy(f32[2,32,128]{2,1,0:T(8,128)S(1)} %get-tuple-element.5) | data formatting | bytes 65536
Async XLA Ops:
  1.3 1.0 %copy-start = (f32[1,3,2,128,128]{4,3,2,1,0:T(8,128)S(1)}, f32[1,3,2,128,128]{4,3,2,1,0:T(8,128)}, u32[]{:S(2)}) copy-start(f32[1,3,2,128,128]{4,3,2,1,0:T(8,128)} %shapes_ref.1) | copy-start | bytes 1179652
  2.3 0.8 %copy-start.1 = (f32[2,32,128]{2,1,0:T(8,128)S(1)}, f32[2,32,128]{2,1,0:T(8,128)}, u32[]{:S(2)}) copy-start(f32[2,32,128]{2,1,0:T(8,128)} %design_ref.1) | copy-start | bytes 98308

commit v2 on v1

--- a/solution.py
+++ b/solution.py
@@ -25,6 +25,7 @@
 LAME = POISSON / ((1.0 + POISSON) * (1.0 - 2.0 * POISSON))
 SHEAR = 0.5 / (1.0 + POISSON)
 MESH = pl.DeviceIdType.MESH
+DIRECT_LIMIT = 64
 DIRECTIONS = [(dx, dy) for dx in (-1, 0, 1) for dy in (-1, 0, 1) if (dx, dy) != (0, 0)]
 
 
@@ -121,50 +122,77 @@
 
 def kernel(
     slabs, groups,
-    design_ref, shapes_ref, eig_ref, sens_ref, new_ref,
-    design_ext, grad_ext, plane, outgoing, incoming, weight_tiles, partial, row_tiles, column_tiles, trial_rows,
-    design_sems, grad_sems, plane_sems, form_sems, weight_sems, row_sems, column_sems,
+    design_hbm, shapes_hbm, eig_ref, sens_ref, new_ref,
+    design_ref, shapes_ref, design_ext, grad_ext, plane, outgoing, incoming, weight_tiles, partial,
+    row_tiles, column_tiles, trial_rows,
+    load_sems, design_sems, grad_sems, plane_sems, form_sems, weight_sems, row_sems, column_sems,
 ):
     cells, rows, depth = design_ref.shape
     modes, node_rows = shapes_ref.shape[0], shapes_ref.shape[3]
     total_x, total_rows = cells * slabs, rows * groups
     s, m = lax.axis_index("slab"), lax.axis_index("mode")
+    me, devices = s * groups + m, slabs * groups
+    direct = devices <= DIRECT_LIMIT
     sub = 16 if rows % 16 == 0 else 8
 
+    load_shapes = pltpu.make_async_copy(shapes_hbm, shapes_ref, load_sems.at[0])
+    load_design = pltpu.make_async_copy(design_hbm, design_ref, load_sems.at[1])
+    load_shapes.start()
+    load_design.start()
     design_ext[...] = jnp.zeros_like(design_ext)
     grad_ext[...] = jnp.zeros_like(grad_ext)
 
-    @pl.when(s == slabs - 1)
-    def _():
-        plane[...] = jnp.zeros_like(plane)
-
     barrier = pltpu.get_barrier_semaphore()
-    expected = (groups - 1) + (slabs - 1)
-    for d in range(1, groups):
-        pl.semaphore_signal(barrier, inc=1, device_id=(s, lax.rem(m + d, groups)), device_id_type=MESH)
-    for d in range(1, slabs):
-        pl.semaphore_signal(barrier, inc=1, device_id=(lax.rem(s + d, slabs), m), device_id_type=MESH)
-    for dx, dy in DIRECTIONS:
-        if dx and dy:
-            fits = (s + dx >= 0) & (s + dx < slabs) & (m + dy >= 0) & (m + dy < groups)
-            expected = expected + fits.astype(jnp.int32)
-
-            @pl.when(fits)
-            def _():
-                pl.semaphore_signal(barrier, inc=1, device_id=(s + dx, m + dy), device_id_type=MESH)
-
-    pl.semaphore_wait(barrier, expected)
-
-    def plane_copy():
+
+    def greet(x, y):
+        pl.semaphore_signal(barrier, inc=1, device_id=(x, y), device_id_type=MESH)
+
+    if direct:
+        expected = devices - 1
+        for d in range(1, devices):
+            peer = lax.rem(me + d, devices)
+            greet(peer // groups, lax.rem(peer, groups))
+    else:
+        expected = (groups - 1) + (slabs - 1)
+        for d in range(1, groups):
+            greet(s, lax.rem(m + d, groups))
+        for d in range(1, slabs):
+            greet(lax.rem(s + d, slabs), m)
+        for dx, dy in DIRECTIONS:
+            if dx and dy:
+                fits = (s + dx >= 0) & (s + dx < slabs) & (m + dy >= 0) & (m + dy < groups)
+                expected = expected + fits.astype(jnp.int32)
+
+                @pl.when(fits)
+                def _():
+                    greet(s + dx, m + dy)
+
+    def plane_copy(piece):
+        if piece == groups:
+            start, count = m * rows, PAD
+        elif piece == 0:
+            start, count = m * rows + PAD, rows - PAD
+        else:
+            start, count = lax.rem(m + piece, groups) * rows, rows
+        at = pl.ds(pl.multiple_of(start, 8), count)
         return pltpu.make_async_remote_copy(
-            src_ref=shapes_ref.at[:, :, 0], dst_ref=plane,
-            send_sem=plane_sems.at[0], recv_sem=plane_sems.at[1],
+            src_ref=shapes_ref.at[:, :, 0, at], dst_ref=plane.at[:, :, at],
+            send_sem=plane_sems.at[0, piece], recv_sem=plane_sems.at[1, piece],
             device_id=(s - 1, m), device_id_type=MESH,
         )
 
-    @pl.when(s > 0)
-    def _():
-        plane_copy().start()
+    pieces = list(range(1, groups)) + [groups] + ([0] if rows > PAD else [])
+
+    def each_piece(action):
+        here = s < slabs - 1 if action == "wait_recv" else s > 0
+
+        def run(some):
+            @pl.when(here)
+            def _():
+                for piece in some:
+                    getattr(plane_copy(piece), action)()
+
+        return run
 
     def halo(source, x_off, y_off, target, sems, number):
         dx, dy = DIRECTIONS[number]
@@ -213,10 +241,22 @@
             for d in range(1, slabs)
         ]
 
+    def all_exchange(buffer, sems):
+        copies = []
+        for d in range(1, devices):
+            peer = lax.rem(me + d, devices)
+            copies.append(
+                pltpu.make_async_remote_copy(
+                    src_ref=buffer.at[me], dst_ref=buffer.at[me],
+                    send_sem=sems.at[0], recv_sem=sems.at[1],
+                    device_id=(peer // groups, lax.rem(peer, groups)), device_id_type=MESH,
+                )
+            )
+        others = buffer.at[pl.ds(0, devices - 1)]
+        waits = [pltpu.make_async_copy(others, others, sems.at[i]) for i in range(2)]
+        return copies, waits
+
     weight_copies = mode_exchange(weight_tiles, weight_sems)
-    for copy in weight_copies:
-        copy.start()
-    design_halo("start", 1)
 
     def node_view(mode, comp, layer):
         if layer == cells:
@@ -254,25 +294,42 @@
         )
 
     order = list(range(1, groups)) + [0]
-    for layer in range(cells):
-        if layer == cells - 1:
-            design_ext[MARGIN : MARGIN + cells, PAD : PAD + rows, :] = design_ref[...]
-            x_tables = [axis_tables(jnp.full((1, depth), s * cells + i, jnp.int32), total_x) for i in range(cells)]
-            y_tables = axis_tables(m * rows + lax.broadcasted_iota(jnp.int32, (rows, depth), 0), total_rows)
-            z_tables = axis_tables(lax.broadcasted_iota(jnp.int32, (1, depth), 1), depth)
-            spans = [x[0] * (y_tables[0] * z_tables[0]) for x in x_tables]
-            measures = [x[1] * (y_tables[1] * z_tables[1]) for x in x_tables]
-            design_halo("wait_recv", -1)
-            densities = [f / span for f, span in zip(filtered(design_ext, cells, rows, depth), spans)]
-
-            @pl.when(s < slabs - 1)
-            def _():
-                plane_copy().wait_recv()
-
+    x_tables = [axis_tables(jnp.full((1, depth), s * cells + i, jnp.int32), total_x) for i in range(cells)]
+    y_tables = axis_tables(m * rows + lax.broadcasted_iota(jnp.int32, (rows, depth), 0), total_rows)
+    z_tables = axis_tables(lax.broadcasted_iota(jnp.int32, (1, depth), 1), depth)
+    spans = [x[0] * (y_tables[0] * z_tables[0]) for x in x_tables]
+    measures = [x[1] * (y_tables[1] * z_tables[1]) for x in x_tables]
+
+    @pl.when(s == slabs - 1)
+    def _():
+        plane[...] = jnp.zeros_like(plane)
+
+    load_shapes.wait()
+    for layer in range(cells - 1):
         for d in order:
             layer_forms(layer, lax.rem(m + d, groups))
-            if d:
-                form_copy(layer, d).start()
+    load_design.wait()
+    pl.semaphore_wait(barrier, expected)
+
+    each_piece("start")(pieces)
+    for layer in range(cells - 1):
+        for d in range(1, groups):
+            form_copy(layer, d).start()
+    for copy in weight_copies:
+        copy.start()
+    design_halo("start", 1)
+    design_ext[MARGIN : MARGIN + cells, PAD : PAD + rows, :] = design_ref[...]
+    design_halo("wait_recv", -1)
+    densities = [f / span for f, span in zip(filtered(design_ext, cells, rows, depth), spans)]
+
+    waiting = list(pieces)
+    for number, d in enumerate(order):
+        ready = len(waiting) if d == 0 else (2 if number == 0 else 1)
+        each_piece("wait_recv")(waiting[:ready])
+        waiting = waiting[ready:]
+        layer_forms(cells - 1, lax.rem(m + d, groups))
+        if d:
+            form_copy(cells - 1, d).start()
 
     for copy in weight_copies:
         copy.wait_recv()
@@ -305,11 +362,11 @@
     def folded(value):
         return jnp.sum(value, axis=0, keepdims=True)
 
-    lane = lax.broadcasted_iota(jnp.int32, (8, depth), 1)
+    lane = lax.broadcasted_iota(jnp.int32, (1, 128), 1)
     low = jnp.full((1, 1), LEVEL_LOW, jnp.float32)
     target = None
     width = LEVEL_HIGH - LEVEL_LOW
-    copies = []
+    sends = [copy.wait_send for copy in weight_copies]
     for turn in range(2):
         width = width / TRIALS
         trial_rows[0] = scale * jnp.exp(-0.5 * low)
@@ -324,28 +381,38 @@
             partial[trial : trial + 8, :] = jnp.concatenate(lines, 0)
         if turn == 0:
             partial[TRIALS:, :] = jnp.zeros((partial.shape[0] - TRIALS, depth), jnp.float32)
-        row_tiles[turn, m] = lax.dot_general(
+        summed = lax.dot_general(
             jnp.ones((8, depth), jnp.float32), partial[...], (((1,), (1,)), ((), ())),
             precision=lax.Precision.HIGHEST, preferred_element_type=jnp.float32,
         )
-        across = mode_exchange(row_tiles.at[turn], row_sems.at[turn])
-        for copy in across:
-            copy.start()
-        for copy in across:
-            copy.wait_recv()
-        column_tiles[turn, s] = total_of([row_tiles[turn, i] for i in range(groups)])
-        along = slab_exchange(column_tiles.at[turn], column_sems.at[turn])
-        for copy in along:
-            copy.start()
-        for copy in along:
-            copy.wait_recv()
-        copies += across + along
-        volumes = total_of([column_tiles[turn, i] for i in range(slabs)])
+        if direct:
+            row_tiles[turn, me] = summed[0:1]
+            copies, waits = all_exchange(row_tiles.at[turn], row_sems.at[turn])
+            for copy in copies:
+                copy.start()
+            waits[1].wait()
+            sends.append(waits[0].wait)
+            volumes = total_of([row_tiles[turn, i] for i in range(devices)])
+        else:
+            row_tiles[turn, m] = summed[0:1]
+            across = mode_exchange(row_tiles.at[turn], row_sems.at[turn])
+            for copy in across:
+                copy.start()
+            for copy in across:
+                copy.wait_recv()
+            column_tiles[turn, s] = total_of([row_tiles[turn, i] for i in range(groups)])
+            along = slab_exchange(column_tiles.at[turn], column_sems.at[turn])
+            for copy in along:
+                copy.start()
+            for copy in along:
+                copy.wait_recv()
+            sends += [copy.wait_send for copy in across + along]
+            volumes = total_of([column_tiles[turn, i] for i in range(slabs)])
         if turn == 0:
             target = volumes[:, 0:1]
         above = (volumes > target) & (lane >= 1) & (lane < TRIALS)
         count = jnp.sum(jnp.where(above, 1.0, 0.0), axis=1, keepdims=True)
-        low = low + count[0:1] * width
+        low = low + count * width
     shrink = jnp.exp(-0.5 * (low + 0.5 * width))
     for cell in range(cells):
         design = design_ref[cell]
@@ -355,12 +422,9 @@
             jnp.minimum(design + MOVE_LIMIT, 1.0),
         )
 
-    @pl.when(s > 0)
-    def _():
-        plane_copy().wait_send()
-
-    for copy in copies + weight_copies:
-        copy.wait_send()
+    each_piece("wait_send")(pieces)
+    for wait in sends:
+        wait()
     for layer in range(cells):
         for d in range(1, groups):
             form_copy(layer, d).wait_send()
@@ -375,23 +439,26 @@
     ext = pltpu.VMEM((cells + 2 * MARGIN, rows + 2 * PAD, depth), f32)
     forms = pltpu.VMEM((groups, cells, 2, rows, depth), f32)
     dma = pltpu.SemaphoreType.DMA
-    vmem = pl.BlockSpec(memory_space=pltpu.VMEM)
+    vmem, hbm = [pl.BlockSpec(memory_space=space) for space in (pltpu.VMEM, pltpu.HBM)]
+    devices = slabs * groups
+    direct = devices <= DIRECT_LIMIT
     return pl.pallas_call(
         functools.partial(kernel, slabs, groups),
         out_shape=[jax.ShapeDtypeStruct(design.shape, f32)] * 2,
-        in_specs=[vmem, vmem, pl.BlockSpec(memory_space=pltpu.SMEM)],
+        in_specs=[hbm, hbm, pl.BlockSpec(memory_space=pltpu.SMEM)],
         out_specs=[vmem, vmem],
         scratch_shapes=[
+            pltpu.VMEM(design.shape, f32), pltpu.VMEM(mode_shapes.shape, f32),
             ext, ext,
             pltpu.VMEM((modes, 3, node_rows, depth), f32),
             forms, forms,
             pltpu.VMEM((groups, 8, depth), f32),
             pltpu.VMEM((128, depth), f32),
-            pltpu.VMEM((2, groups, 8, 128), f32),
-            pltpu.VMEM((2, slabs, 8, 128), f32),
+            pltpu.VMEM((2, devices if direct else groups, 1, 128), f32),
+            pltpu.VMEM((2, slabs, 1, 128), f32),
             pltpu.VMEM((3, cells * rows, depth), f32),
-            dma((2, len(DIRECTIONS))), dma((2, len(DIRECTIONS))), dma((2,)),
-            dma((2, cells, groups)), dma((2, groups)), dma((2, 2, groups)), dma((2, 2, slabs)),
+            dma((2,)), dma((2, len(DIRECTIONS))), dma((2, len(DIRECTIONS))), dma((2, groups + 1)),
+            dma((2, cells, groups)), dma((2, groups)), dma((2, 2) if direct else (2, 2, groups)), dma((2, 2, slabs)),
         ],
         compiler_params=pltpu.CompilerParams(
             collective_id=0, has_side_effects=True, vmem_limit_bytes=32 * 1024 * 1024

time: 41 us -> 38 us (0.927)
  Pallas kernels: 36.5 us -> 33.5 us
    pallas_call x1, Pallas kernels: 36.5 us -> 33.5 us  [local(): pl.pallas_call(functools.partial(kernel, slabs, groups), out_shape=[jax.S...]
where the time goes in v2:
time: 38 us; the launch traced here: 37.8 us
  Pallas kernels  33.5 us (88%)
  local copies, waits for them, and re-layouts  2.98 us (8%)
  between operations  1.29 us (3%)
    pallas_call x1, Pallas kernels, local(): pl.pallas_call(functools.partial(kernel, slabs, groups), out_shape=[jax.S...  33.5 us
    unnamed x6, local copies, waits for them, and re-layouts  2.98 us

profile of v2, /device:TPU:0, one launch (start us, length us, event | category | flops | bytes accessed | tf_op | source)
XLA Modules:
  0.0 37.8 jit_solution(5722600759307282186)
XLA Ops:
  1.3 0.0 copy-start
  1.3 1.0 %copy-done = f32[1,3,2,128,128]{4,3,2,1,0:T(8,128)S(1)} copy-done((f32[1,3,2,128,128]{4,3,2,1,0:T(8,128)S(1)}, f32[1,3,2,128,128]{4,3,2,1,0:T(8,128)}, u32[]{:S(2)}) %copy-start) | copy-done | bytes 393240
  2.3 0.0 copy-start.1
  2.3 0.8 %copy-done.1 = f32[2,32,128]{2,1,0:T(8,128)S(1)} copy-done((f32[2,32,128]{2,1,0:T(8,128)S(1)}, f32[2,32,128]{2,1,0:T(8,128)}, u32[]{:S(2)}) %copy-start.1) | copy-done | bytes 32792
  3.0 33.5 %shard_map.50 = (f32[2,32,128]{2,1,0:T(8,128)S(1)}, f32[2,32,128]{2,1,0:T(8,128)S(1)}) custom-call(f32[2,32,128]{2,1,0:T(8,128)S(1)} %copy-done.1, f32[1,3,2,128,128]{4,3,2,1,0:T(8,128)S(1)} %copy-done, f32[1]{0:T(128)S(6)} %copy.7.eig_ref), custom_call_target="tpu_custom_call" | custom-call | tf_op jit(solution)/shard_map/pallas_call | solution.py:445
  36.5 0.6 %copy.8 = f32[2,32,128]{2,1,0:T(8,128)} copy(f32[2,32,128]{2,1,0:T(8,128)S(1)} %get-tuple-element.4) | data formatting | bytes 65536
  37.2 0.6 %copy.9 = f32[2,32,128]{2,1,0:T(8,128)} copy(f32[2,32,128]{2,1,0:T(8,128)S(1)} %get-tuple-element.5) | data formatting | bytes 65536
Async XLA Ops:
  1.3 1.0 %copy-start = (f32[1,3,2,128,128]{4,3,2,1,0:T(8,128)S(1)}, f32[1,3,2,128,128]{4,3,2,1,0:T(8,128)}, u32[]{:S(2)}) copy-start(f32[1,3,2,128,128]{4,3,2,1,0:T(8,128)} %shapes_hbm.1) | copy-start | bytes 1179652
  2.3 0.8 %copy-start.1 = (f32[2,32,128]{2,1,0:T(8,128)S(1)}, f32[2,32,128]{2,1,0:T(8,128)}, u32[]{:S(2)}) copy-start(f32[2,32,128]{2,1,0:T(8,128)} %design_hbm.1) | copy-start | bytes 98308

commit v3 on v2

--- a/solution.py
+++ b/solution.py
@@ -133,6 +133,10 @@
     s, m = lax.axis_index("slab"), lax.axis_index("mode")
     me, devices = s * groups + m, slabs * groups
     direct = devices <= DIRECT_LIMIT
+    xs = [s] + [jnp.where(s + d >= slabs, s + d - slabs, s + d) for d in range(1, slabs)]
+    ys = [m] + [jnp.where(m + d >= groups, m + d - groups, m + d) for d in range(1, groups)]
+    far_first = sorted(range(slabs), key=lambda d: abs(2 * d - slabs))
+    peers = [(xs[dx], ys[dy]) for dx in far_first for dy in range(groups) if dx or dy]
     sub = 16 if rows % 16 == 0 else 8
 
     load_shapes = pltpu.make_async_copy(shapes_hbm, shapes_ref, load_sems.at[0])
@@ -149,15 +153,14 @@
 
     if direct:
         expected = devices - 1
-        for d in range(1, devices):
-            peer = lax.rem(me + d, devices)
-            greet(peer // groups, lax.rem(peer, groups))
+        for peer in peers:
+            greet(*peer)
     else:
         expected = (groups - 1) + (slabs - 1)
         for d in range(1, groups):
-            greet(s, lax.rem(m + d, groups))
+            greet(s, ys[d])
         for d in range(1, slabs):
-            greet(lax.rem(s + d, slabs), m)
+            greet(xs[d], m)
         for dx, dy in DIRECTIONS:
             if dx and dy:
                 fits = (s + dx >= 0) & (s + dx < slabs) & (m + dy >= 0) & (m + dy < groups)
@@ -173,7 +176,7 @@
         elif piece == 0:
             start, count = m * rows + PAD, rows - PAD
         else:
-            start, count = lax.rem(m + piece, groups) * rows, rows
+            start, count = ys[piece] * rows, rows
         at = pl.ds(pl.multiple_of(start, 8), count)
         return pltpu.make_async_remote_copy(
             src_ref=shapes_ref.at[:, :, 0, at], dst_ref=plane.at[:, :, at],
@@ -226,7 +229,7 @@
             pltpu.make_async_remote_copy(
                 src_ref=buffer.at[m], dst_ref=buffer.at[m],
                 send_sem=sems.at[0, d], recv_sem=sems.at[1, d],
-                device_id=(s, lax.rem(m + d, groups)), device_id_type=MESH,
+                device_id=(s, ys[d]), device_id_type=MESH,
             )
             for d in range(1, groups)
         ]
@@ -236,20 +239,19 @@
             pltpu.make_async_remote_copy(
                 src_ref=buffer.at[s], dst_ref=buffer.at[s],
                 send_sem=sems.at[0, d], recv_sem=sems.at[1, d],
-                device_id=(lax.rem(s + d, slabs), m), device_id_type=MESH,
+                device_id=(xs[d], m), device_id_type=MESH,
             )
             for d in range(1, slabs)
         ]
 
     def all_exchange(buffer, sems):
         copies = []
-        for d in range(1, devices):
-            peer = lax.rem(me + d, devices)
+        for peer in peers:
             copies.append(
                 pltpu.make_async_remote_copy(
                     src_ref=buffer.at[me], dst_ref=buffer.at[me],
                     send_sem=sems.at[0], recv_sem=sems.at[1],
-                    device_id=(peer // groups, lax.rem(peer, groups)), device_id_type=MESH,
+                    device_id=peer, device_id_type=MESH,
                 )
             )
         others = buffer.at[pl.ds(0, devices - 1)]
@@ -286,7 +288,7 @@
         lax.fori_loop(0, rows // sub, step, 0)
 
     def form_copy(layer, d):
-        group = lax.rem(m + d, groups)
+        group = ys[d]
         return pltpu.make_async_remote_copy(
             src_ref=outgoing.at[group, layer], dst_ref=incoming.at[d, layer],
             send_sem=form_sems.at[0, layer, d], recv_sem=form_sems.at[1, layer, d],
@@ -307,7 +309,7 @@
     load_shapes.wait()
     for layer in range(cells - 1):
         for d in order:
-            layer_forms(layer, lax.rem(m + d, groups))
+            layer_forms(layer, ys[d])
     load_design.wait()
     pl.semaphore_wait(barrier, expected)
 
@@ -319,18 +321,18 @@
         copy.start()
     design_halo("start", 1)
     design_ext[MARGIN : MARGIN + cells, PAD : PAD + rows, :] = design_ref[...]
-    design_halo("wait_recv", -1)
-    densities = [f / span for f, span in zip(filtered(design_ext, cells, rows, depth), spans)]
 
     waiting = list(pieces)
     for number, d in enumerate(order):
         ready = len(waiting) if d == 0 else (2 if number == 0 else 1)
         each_piece("wait_recv")(waiting[:ready])
         waiting = waiting[ready:]
-        layer_forms(cells - 1, lax.rem(m + d, groups))
+        layer_forms(cells - 1, ys[d])
         if d:
             form_copy(cells - 1, d).start()
 
+    design_halo("wait_recv", -1)
+    densities = [f / span for f, span in zip(filtered(design_ext, cells, rows, depth), spans)]
     for copy in weight_copies:
         copy.wait_recv()
     weight_total = total_of([weight_tiles[i] for i in range(groups)])[0:1]

time: 38 us -> 34.7 us (0.913)
  Pallas kernels: 33.5 us -> 30.2 us
    pallas_call x1, Pallas kernels: 33.5 us -> 30.2 us  [local(): pl.pallas_call(functools.partial(kernel, slabs, groups), out_shape=[jax.S...]
where the time goes in v3:
time: 34.7 us; the launch traced here: 34.4 us
  Pallas kernels  30.2 us (87%)
  local copies, waits for them, and re-layouts  2.98 us (9%)
  between operations  1.29 us (4%)
    pallas_call x1, Pallas kernels, local(): pl.pallas_call(functools.partial(kernel, slabs, groups), out_shape=[jax.S...  30.2 us
    unnamed x6, local copies, waits for them, and re-layouts  2.98 us

profile of v3, /device:TPU:0, one launch (start us, length us, event | category | flops | bytes accessed | tf_op | source)
XLA Modules:
  0.0 34.4 jit_solution(15158896353303942829)
XLA Ops:
  1.3 0.0 copy-start
  1.3 1.0 %copy-done = f32[1,3,2,128,128]{4,3,2,1,0:T(8,128)S(1)} copy-done((f32[1,3,2,128,128]{4,3,2,1,0:T(8,128)S(1)}, f32[1,3,2,128,128]{4,3,2,1,0:T(8,128)}, u32[]{:S(2)}) %copy-start) | copy-done | bytes 393240
  2.3 0.0 copy-start.1
  2.3 0.8 %copy-done.1 = f32[2,32,128]{2,1,0:T(8,128)S(1)} copy-done((f32[2,32,128]{2,1,0:T(8,128)S(1)}, f32[2,32,128]{2,1,0:T(8,128)}, u32[]{:S(2)}) %copy-start.1) | copy-done | bytes 32792
  3.0 30.2 %shard_map.50 = (f32[2,32,128]{2,1,0:T(8,128)S(1)}, f32[2,32,128]{2,1,0:T(8,128)S(1)}) custom-call(f32[2,32,128]{2,1,0:T(8,128)S(1)} %copy-done.1, f32[1,3,2,128,128]{4,3,2,1,0:T(8,128)S(1)} %copy-done, f32[1]{0:T(128)S(6)} %copy.7.eig_ref), custom_call_target="tpu_custom_call" | custom-call | tf_op jit(solution)/shard_map/pallas_call | solution.py:447
  33.2 0.6 %copy.8 = f32[2,32,128]{2,1,0:T(8,128)} copy(f32[2,32,128]{2,1,0:T(8,128)S(1)} %get-tuple-element.4) | data formatting | bytes 65536
  33.8 0.6 %copy.9 = f32[2,32,128]{2,1,0:T(8,128)} copy(f32[2,32,128]{2,1,0:T(8,128)S(1)} %get-tuple-element.5) | data formatting | bytes 65536
Async XLA Ops:
  1.3 1.0 %copy-start = (f32[1,3,2,128,128]{4,3,2,1,0:T(8,128)S(1)}, f32[1,3,2,128,128]{4,3,2,1,0:T(8,128)}, u32[]{:S(2)}) copy-start(f32[1,3,2,128,128]{4,3,2,1,0:T(8,128)} %shapes_hbm.1) | copy-start | bytes 1179652
  2.3 0.8 %copy-start.1 = (f32[2,32,128]{2,1,0:T(8,128)S(1)}, f32[2,32,128]{2,1,0:T(8,128)}, u32[]{:S(2)}) copy-start(f32[2,32,128]{2,1,0:T(8,128)} %design_hbm.1) | copy-start | bytes 98308
